TPU v7x, 256 devices: a whole 4x4x8 slice. The times are simulated.
256 devices in a mesh: ctx: 8 (over y_lo, x), resp: 32 (over y_hi, z, core).
Axes of the slice: x: 4, y: 4 (y_hi: 2, y_lo: 2; y = y_hi * 2 + y_lo), z: 8, core: 2. Of those that a mesh axis runs over, the one named last changes fastest.
Arguments:
- resp_query: bfloat16 [32, 1024, 4096], P('resp', 'ctx'), may hold values from -10 to 10
- resp_key: bfloat16 [32, 1024, 512], P('resp', 'ctx'), may hold values from -5 to 5
- resp_value: bfloat16 [32, 1024, 512], P('resp', 'ctx'), may hold values from -6 to 6
- resp_out: bfloat16 [32, 1024, 4096], P('resp', 'ctx'), may hold values from -3 to 3
- resp_grad: bfloat16 [32, 1024, 4096], P('resp', 'ctx'), may hold values from -6 to 6
- pack_query: bfloat16 [512, 4096], P(('ctx', 'resp')), may hold values from -10 to 10
- pack_key: bfloat16 [512, 512], P(('ctx', 'resp')), may hold values from -5 to 5
- pack_value: bfloat16 [512, 512], P(('ctx', 'resp')), may hold values from -6 to 6
- pack_out: bfloat16 [512, 4096], P(('ctx', 'resp')), may hold values from -3 to 3
- pack_grad: bfloat16 [512, 4096], P(('ctx', 'resp')), may hold values from -6 to 6
- resp_length: int32 [32], P('resp'), may hold values from 1 to 1024, as said below
- prompt_id: int32 [32], P('resp'), may hold values from 0 to 1
- pack_offset: int32 [3], replicated, may hold values from 0 to 512, as said below
Outputs:
- resp_query_grad: bfloat16 [32, 1024, 4096], P('resp', 'ctx')
- resp_key_grad: bfloat16 [32, 1024, 512], P('resp', 'ctx')
- resp_value_grad: bfloat16 [32, 1024, 512], P('resp', 'ctx')
- pack_query_grad: bfloat16 [512, 4096], P(('ctx', 'resp'))
- pack_key_grad: bfloat16 [512, 512], P(('ctx', 'resp'))
- pack_value_grad: bfloat16 [512, 512], P(('ctx', 'resp'))
Inputs may be any that keep to these rules, and one draw needn't show every extreme that they name: pack_offset starts at 0, rises strictly and ends at 512. `resp_length`: some response has the full length 1024.
All inputs are finite; a program needn't handle non-finite values.
Results may differ from a plain program's by a relative error of at most 0.015.
Values may be sent and summed in bfloat16 or wider, within the bound.
No kernel may reach another device: no remote copies, remote signals or barrier semaphores. Data moves between devices by JAX's collectives and lax.ppermute only.
A program may use at most 128 MiB of HBM per device.

v0:
```python
import jax
import jax.numpy as jnp
from jax import lax
from jax.sharding import PartitionSpec as P

HQ = 32
KEY_VALUE_HEADS = 4
HEAD_SIZE = 128
GROUP = 8
PROMPTS = 2


def attend(queries, cotangent, output, all_keys, all_values, key_mask):
    row_count = queries.shape[0]
    key_count = all_keys.shape[0]
    score_scale = HEAD_SIZE ** (-0.5)
    query_heads = queries.reshape(row_count, KEY_VALUE_HEADS, GROUP, HEAD_SIZE)
    grad_heads = cotangent.reshape(row_count, KEY_VALUE_HEADS, GROUP, HEAD_SIZE)
    out_heads = output.reshape(row_count, KEY_VALUE_HEADS, GROUP, HEAD_SIZE)
    key_heads = all_keys.reshape(key_count, KEY_VALUE_HEADS, HEAD_SIZE)
    value_heads = all_values.reshape(key_count, KEY_VALUE_HEADS, HEAD_SIZE)
    row_delta = jnp.sum(grad_heads.astype(jnp.float32) * out_heads.astype(jnp.float32), axis=-1)
    query_list, key_list, value_list = ([], [], [])
    for kv_head in range(KEY_VALUE_HEADS):
        scores = (
            jnp.einsum(
                "rgd,jd->grj",
                query_heads[:, kv_head],
                key_heads[:, kv_head],
                preferred_element_type=jnp.float32,
            )
            * score_scale
        )
        scores = jnp.where(key_mask[None], scores, -jnp.inf)
        row_top = jnp.max(scores, axis=-1, keepdims=True)
        row_total = jnp.sum(jnp.exp(scores - row_top), axis=-1, keepdims=True)
        softmax_prob = jnp.exp(scores - (row_top + jnp.log(row_total)))
        weights = softmax_prob.astype(jnp.bfloat16)
        grad_prob = jnp.einsum(
            "rgd,jd->grj",
            grad_heads[:, kv_head],
            value_heads[:, kv_head],
            preferred_element_type=jnp.float32,
        )
        shift_delta = jnp.transpose(row_delta[:, kv_head])[:, :, None]
        dscore = (softmax_prob * (grad_prob - shift_delta)).astype(jnp.bfloat16)
        query_list.append(
            jnp.einsum(
                "grj,jd->rgd", dscore, key_heads[:, kv_head], preferred_element_type=jnp.float32
            )
            * score_scale
        )
        key_list.append(
            jnp.einsum(
                "grj,rgd->jd", dscore, query_heads[:, kv_head], preferred_element_type=jnp.float32
            )
            * score_scale
        )
        value_list.append(
            jnp.einsum(
                "grj,rgd->jd", weights, grad_heads[:, kv_head], preferred_element_type=jnp.float32
            )
        )
    query_grad = jnp.stack(query_list, axis=1).reshape(row_count, HQ * HEAD_SIZE)
    key_grad = jnp.stack(key_list, axis=1).reshape(key_count, KEY_VALUE_HEADS * HEAD_SIZE)
    value_gradient = jnp.stack(value_list, axis=1).reshape(key_count, KEY_VALUE_HEADS * HEAD_SIZE)
    return (query_grad, key_grad, value_gradient)


def prompt_of(positions, pack_offset):
    return jnp.sum((positions[:, None] >= pack_offset[None, 1:PROMPTS]).astype(jnp.int32), axis=1)


def shards(
    resp_query,
    resp_key,
    resp_value,
    resp_out,
    resp_grad,
    pack_query,
    pack_key,
    pack_value,
    pack_out,
    pack_grad,
    resp_length,
    prompt_id,
    pack_offset,
):
    resp_count = lax.axis_size("resp")
    ctx_index = lax.axis_index("ctx")
    resp_index = lax.axis_index("resp")
    rows_resp = resp_query.shape[1]
    rows_pack = pack_query.shape[0]
    block_key, block_value = (
        lax.all_gather(pack_key, "resp", axis=0, tiled=True),
        lax.all_gather(pack_value, "resp", axis=0, tiled=True),
    )
    whole_key, whole_value = (
        lax.all_gather(block_key, "ctx", axis=0, tiled=True),
        lax.all_gather(block_value, "ctx", axis=0, tiled=True),
    )
    total_pack = whole_key.shape[0]
    own_key, own_value = (
        lax.all_gather(resp_key[0], "ctx", axis=0, tiled=True),
        lax.all_gather(resp_value[0], "ctx", axis=0, tiled=True),
    )
    total_resp = own_key.shape[0]
    position = jnp.arange(total_pack, dtype=jnp.int32)
    pack_prompt = prompt_of(position, pack_offset)
    pack_rows = (ctx_index * resp_count + resp_index) * rows_pack + jnp.arange(
        rows_pack, dtype=jnp.int32
    )
    row_prompt = prompt_of(pack_rows, pack_offset)
    pack_mask = (row_prompt[:, None] == pack_prompt[None, :]) & (
        position[None, :] <= pack_rows[:, None]
    )
    pack_qgrad, pack_kgrad, pack_vgrad = attend(
        pack_query, pack_grad, pack_out, whole_key, whole_value, pack_mask
    )
    resp_rows = ctx_index * rows_resp + jnp.arange(rows_resp, dtype=jnp.int32)
    live_rows = (resp_rows < resp_length[0])[:, None]
    live_grad = jnp.where(live_rows, resp_grad[0], jnp.zeros_like(resp_grad[0]))
    all_keys = jnp.concatenate([whole_key, own_key], axis=0)
    all_values = jnp.concatenate([whole_value, own_value], axis=0)
    prefix_mask = jnp.broadcast_to((pack_prompt == prompt_id[0])[None, :], (rows_resp, total_pack))
    causal = jnp.arange(total_resp, dtype=jnp.int32)[None, :] <= resp_rows[:, None]
    key_mask = jnp.concatenate([prefix_mask, causal], axis=1)
    resp_qgrad, mixed_kgrad, mixed_vgrad = attend(
        resp_query[0], live_grad, resp_out[0], all_keys, all_values, key_mask
    )
    prefix_kgrad = pack_kgrad + mixed_kgrad[:total_pack]
    prefix_vgrad = pack_vgrad + mixed_vgrad[:total_pack]
    owned_kgrad, owned_vgrad = (
        lax.psum_scatter(prefix_kgrad, ("ctx", "resp"), scatter_dimension=0, tiled=True),
        lax.psum_scatter(prefix_vgrad, ("ctx", "resp"), scatter_dimension=0, tiled=True),
    )
    own_kgrad, own_vgrad = (
        lax.psum_scatter(
            mixed_kgrad[total_pack:].astype(jnp.bfloat16), "ctx", scatter_dimension=0, tiled=True
        ).astype(jnp.float32),
        lax.psum_scatter(
            mixed_vgrad[total_pack:].astype(jnp.bfloat16), "ctx", scatter_dimension=0, tiled=True
        ).astype(jnp.float32),
    )
    return (
        resp_qgrad.astype(jnp.bfloat16)[None],
        own_kgrad.astype(jnp.bfloat16)[None],
        own_vgrad.astype(jnp.bfloat16)[None],
        pack_qgrad.astype(jnp.bfloat16),
        owned_kgrad.astype(jnp.bfloat16),
        owned_vgrad.astype(jnp.bfloat16),
    )


def solution(mesh):
    placed = (
        P("resp", "ctx", None),
        P("resp", "ctx", None),
        P("resp", "ctx", None),
        P("resp", "ctx", None),
        P("resp", "ctx", None),
        P(("ctx", "resp"), None),
        P(("ctx", "resp"), None),
        P(("ctx", "resp"), None),
        P(("ctx", "resp"), None),
        P(("ctx", "resp"), None),
        P("resp"),
        P("resp"),
        P(),
    )
    return jax.shard_map(
        shards,
        mesh=mesh,
        in_specs=placed,
        out_specs=(
            P("resp", "ctx", None),
            P("resp", "ctx", None),
            P("resp", "ctx", None),
            P(("ctx", "resp"), None),
            P(("ctx", "resp"), None),
            P(("ctx", "resp"), None),
        ),
        check_vma=False,
    )
```

profile of v0, /device:TPU:1, one launch (start us, length us, event | category | flops | bytes accessed | tf_op | source)
XLA Modules:
  0.0 353.0 jit_solution(2483207960852207233)
XLA Ops:
  14.0 46.6 %all-gather.2 = bf16[32,2,512]{2,1,0:T(2,128)(2,1)S(1)} all-gather(bf16[1,2,512]{2,1,0:T(2,128)(2,1)} %bitcast.588), channel_id=1, replica_groups=mesh['ctx'=8,'resp'=32] {'resp'}, dimensions={0}, use_global_device_ids=true | all-gather | bytes 67584 | tf_op jit(solution)/shard_map/all_gather | solution.py:95
  60.7 23.1 %all_gather.19 = bf16[512,512]{1,0:T(8,128)(2,1)S(1)} all-gather(bf16[64,512]{1,0:T(8,128)(2,1)S(1)} %reshape.246), channel_id=1, replica_groups=mesh['ctx'=8,'resp'=32] {'ctx'}, dimensions={0}, use_global_device_ids=true | all-gather | bytes 589824 | tf_op jit(solution)/shard_map/all_gather | solution.py:99
  85.1 43.0 %all-gather.3 = bf16[32,2,512]{2,1,0:T(2,128)(2,1)S(1)} all-gather(bf16[1,2,512]{2,1,0:T(2,128)(2,1)S(1)} %bitcast.589), channel_id=1, replica_groups=mesh['ctx'=8,'resp'=32] {'resp'}, dimensions={0}, use_global_device_ids=true | all-gather | bytes 67584 | tf_op jit(solution)/shard_map/all_gather | solution.py:96
  128.1 22.9 %all_gather.22 = bf16[512,512]{1,0:T(8,128)(2,1)S(1)} all-gather(bf16[64,512]{1,0:T(8,128)(2,1)S(1)} %reshape.248), channel_id=1, replica_groups=mesh['ctx'=8,'resp'=32] {'ctx'}, dimensions={0}, use_global_device_ids=true | all-gather | bytes 589824 | tf_op jit(solution)/shard_map/all_gather | solution.py:100
  169.2 1.9 multiply_reduce_fusion
  174.3 3.6 %fusion.104 = (f32[8,128]{1,0:T(8,128)S(1)}, f32[8,128,1536]{1,2,0:T(8,128)}) fusion(bf16[128,4,8,128]{0,3,2,1:T(8,128)(2,1)S(1)} %bitcast.562, bf16[1536,4,128]{0,2,1:T(8,128)(2,1)S(1)} %bitcast.531, pred[128,1536]{0,1:T(8,128)(4,1)S(1)} %pad_add_fusion), kind=kOutput, calls=%fused_computation.213 | convolution fusion | flops 407370752 | bytes 7147520 | tf_op jit(solution)/shard_map/rgd,jd->grj/dot_general | solution.py:26
  177.9 3.6 %fusion.105 = (f32[8,128]{1,0:T(8,128)S(1)}, f32[8,128,1536]{1,2,0:T(8,128)}) fusion(bf16[128,4,8,128]{0,3,2,1:T(8,128)(2,1)S(1)} %bitcast.563, bf16[1536,4,128]{0,2,1:T(8,128)(2,1)S(1)} %bitcast.532, pred[128,1536]{0,1:T(8,128)(4,1)S(1)} %pad_add_fusion), kind=kOutput, calls=%fused_computation.214 | convolution fusion | flops 407370752 | bytes 7147520 | tf_op jit(solution)/shard_map/rgd,jd->grj/dot_general | solution.py:26
  181.5 3.6 %fusion.106 = (f32[8,128]{1,0:T(8,128)S(1)}, f32[8,128,1536]{1,2,0:T(8,128)}) fusion(bf16[128,4,8,128]{0,3,2,1:T(8,128)(2,1)S(1)} %bitcast.564, bf16[1536,4,128]{0,2,1:T(8,128)(2,1)S(1)} %bitcast.533, pred[128,1536]{0,1:T(8,128)(4,1)S(1)} %pad_add_fusion), kind=kOutput, calls=%fused_computation.215 | convolution fusion | flops 407370752 | bytes 7147520 | tf_op jit(solution)/shard_map/rgd,jd->grj/dot_general | solution.py:26
  185.2 3.7 %fusion.103 = (f32[8,128]{1,0:T(8,128)S(1)}, f32[8,128,1536]{1,2,0:T(8,128)}) fusion(bf16[128,4,8,128]{0,3,2,1:T(8,128)(2,1)S(1)} %bitcast.565, bf16[1536,4,128]{0,2,1:T(8,128)(2,1)S(1)} %bitcast.534, pred[128,1536]{0,1:T(8,128)(4,1)S(1)} %pad_add_fusion), kind=kOutput, calls=%fused_computation.212 | convolution fusion | flops 407370752 | bytes 7147520 | tf_op jit(solution)/shard_map/rgd,jd->grj/dot_general | solution.py:26
  190.4 4.3 %exponential_reduce_fusion.1 = f32[8,128]{1,0:T(8,128)S(1)} fusion(f32[8,128,1536]{1,2,0:T(8,128)} %get-tuple-element.45, f32[8,128]{1,0:T(8,128)S(1)} %get-tuple-element.44), kind=kLoop, calls=%fused_computation.19 | loop fusion | flops 3144704 | bytes 6299648 | tf_op jit(solution)/shard_map/reduce_sum | solution.py:36
  194.7 4.0 %fusion.30 = f32[1536,1,128]{0,2,1:T(8,128)S(1)} fusion(f32[8,128,1536]{1,2,0:T(8,128)} %get-tuple-element.45, f32[8,128]{1,0:T(8,128)S(1)} %log_add_fusion.1, bf16[128,4,8,128]{3,0,2,1:T(8,128)(2,1)S(1)} %get-tuple-element.33), kind=kOutput, calls=%fused_computation.40 | convolution fusion | flops 405798912 | bytes 7344128 | tf_op jit(solution)/shard_map/grj,rgd->jd/dot_general | solution.py:60
  198.7 2.7 fusion.3
  201.4 3.0 fusion.39
  206.8 3.3 fusion.5
  215.8 2.3 copy.230
  218.2 3.2 fusion.41
  221.4 4.6 %fusion.7 = bf16[8,128,1536]{1,2,0:T(8,128)(2,1)S(1)} fusion(f32[8,128,1536]{1,2,0:T(8,128)} %get-tuple-element.49, f32[8,128]{1,0:T(8,128)S(1)} %copy-done.32, f32[8,128]{1,0:T(8,128)S(1)} %log_add_fusion.3, bf16[1536,4,128]{0,2,1:T(8,128)(2,1)} %bitcast.529, bf16[128,4,8,128]{3,0,2,1:T(8,128)(2,1)S(1)} %copy-done.7), kind=kOutput, calls=%fused_computation.14 | convolution fusion | flops 408944640 | bytes 10100736 | tf_op jit(solution)/shard_map/rgd,jd->grj/dot_general | solution.py:39
  227.3 2.7 fusion.1
  233.2 2.3 copy.221
  235.8 2.6 maximum_add_fusion.1
  238.4 2.6 copy.250
  249.2 2.3 copy.252
  251.5 2.3 maximum_add_fusion
  255.4 90.5 %all-reduce.4 = (bf16[512,512]{1,0:T(8,128)(2,1)S(1)}, bf16[512,512]{1,0:T(8,128)(2,1)S(1)}) all-reduce(f32[512,512]{1,0:T(8,128)} %copy.250, f32[512,512]{1,0:T(8,128)S(1)} %copy.251), channel_id=6, replica_groups=mesh['ctx'=8,'resp'=32] {'ctx','resp'}, use_global_device_ids=true, to_apply=%region_20.21.clone | all-reduce | flops 524288 | bytes 3145728
  (194 shorter events, 52.5 us)
Async XLA Ops:
  7.2 77.7 %copy-start.30 = (bf16[2,4096]{1,0:T(2,128)(2,1)S(1)}, bf16[2,4096]{1,0:T(2,128)(2,1)}, u32[]{:S(2)}) copy-start(bf16[2,4096]{1,0:T(2,128)(2,1)} %param.22) | copy-start | bytes 49156
  7.2 77.7 %copy-start.35 = (bf16[2,4096]{1,0:T(2,128)(2,1)S(1)}, bf16[2,4096]{1,0:T(2,128)(2,1)}, u32[]{:S(2)}) copy-start(bf16[2,4096]{1,0:T(2,128)(2,1)} %param.21) | copy-start | bytes 49156
  7.2 77.9 %copy-start.36 = (bf16[2,512]{1,0:T(2,128)(2,1)S(1)}, bf16[2,512]{1,0:T(2,128)(2,1)}, u32[]{:S(2)}) copy-start(bf16[2,512]{1,0:T(2,128)(2,1)} %param.20) | copy-start | bytes 6148
  7.2 165.6 %all-gather.7.cloned.1.call-start = ((), (), s32[]{:S(2)}) async-start(), calls=%async_computation.4 | async-start | bytes 1179648 | tf_op jit(solution)/shard_map/all_gather | solution.py:104
  8.9 179.9 %all-gather.9.cloned.1.call-start = ((), (), s32[]{:S(2)}) async-start(), calls=%async_computation.5 | async-start | bytes 1179648 | tf_op jit(solution)/shard_map/all_gather | solution.py:105
  10.7 335.8 %reduce-scatter.5.cloned.1.call-start = ((), (), s32[]{:S(2)}) async-start(), calls=%async_computation.3 | async-start | bytes 1179648 | tf_op jit(solution)/shard_map/reduce_scatter | solution.py:141
  83.9 78.0 %copy-start.18 = (bf16[512,512]{0,1:T(8,128)(2,1)}, bf16[512,512]{0,1:T(8,128)(2,1)S(1)}, u32[]{:S(2)}) copy-start(bf16[512,512]{0,1:T(8,128)(2,1)S(1)} %copy.185) | copy-start | bytes 1572868
  84.5 78.3 %copy-start.25 = (bf16[1,128,4096]{2,1,0:T(8,128)(2,1)S(1)}, bf16[1,128,4096]{2,1,0:T(8,128)(2,1)}, u32[]{:S(2)}) copy-start(bf16[1,128,4096]{2,1,0:T(8,128)(2,1)} %param.13) | copy-start | bytes 3145732
  151.2 14.5 %copy-start.23 = (bf16[512,512]{0,1:T(8,128)(2,1)}, bf16[512,512]{0,1:T(8,128)(2,1)S(1)}, u32[]{:S(2)}) copy-start(bf16[512,512]{0,1:T(8,128)(2,1)S(1)} %copy.190) | copy-start | bytes 1572868
  171.2 23.5 %copy-start.5 = (bf16[128,4,8,128]{3,0,2,1:T(8,128)(2,1)}, bf16[128,4,8,128]{3,0,2,1:T(8,128)(2,1)S(1)}, u32[]{:S(2)}) copy-start(bf16[128,4,8,128]{3,0,2,1:T(8,128)(2,1)S(1)} %get-tuple-element.33) | copy-start | bytes 3145732
  174.3 10.9 %copy-start.17 = (bf16[1536,512]{0,1:T(8,128)(2,1)}, bf16[1536,512]{0,1:T(8,128)(2,1)S(1)}, u32[]{:S(2)}) copy-start(bf16[1536,512]{0,1:T(8,128)(2,1)S(1)} %pad_maximum_fusion.2) | copy-start | bytes 4718596
  188.9 9.8 %slice-start.8 = ((s8[6291456]{0:T(1024)(128)(4,1)}), s8[4194304]{0:T(1024)(128)(4,1)S(1)}, s32[]{:S(2)}) async-start(s8[6291456]{0:T(1024)(128)(4,1)} %bitcast.525), calls=%async_computation.14 | async-start | bytes 8388608
  190.3 16.5 %copy-start.16 = (bf16[1536,512]{0,1:T(8,128)(2,1)}, bf16[1536,512]{0,1:T(8,128)(2,1)S(1)}, u32[]{:S(2)}) copy-start(bf16[1536,512]{0,1:T(8,128)(2,1)S(1)} %pad_maximum_fusion.3) | copy-start | bytes 4718596
  190.4 8.3 %slice-start.9 = ((s8[6291456]{0:T(1024)(128)(4,1)}), s8[2097152]{0:T(1024)(128)(4,1)S(1)}, s32[]{:S(2)}) async-start(s8[6291456]{0:T(1024)(128)(4,1)} %bitcast.525), calls=%async_computation.15 | async-start | bytes 4194304
  198.6 15.6 %copy-start.8 = (f32[1536,1,128]{0,2,1:T(8,128)}, f32[1536,1,128]{0,2,1:T(8,128)S(1)}, u32[]{:S(2)}) copy-start(f32[1536,1,128]{0,2,1:T(8,128)S(1)} %fusion.30) | copy-start | bytes 2359300
  198.7 5.7 %slice-start.6 = ((s8[6291456]{0:T(1024)(128)(4,1)}), s8[4194304]{0:T(1024)(128)(4,1)S(1)}, s32[]{:S(2)}) async-start(s8[6291456]{0:T(1024)(128)(4,1)} %bitcast.523), calls=%async_computation.12 | async-start | bytes 8388608
  198.7 5.7 %slice-start.7 = ((s8[6291456]{0:T(1024)(128)(4,1)}), s8[2097152]{0:T(1024)(128)(4,1)S(1)}, s32[]{:S(2)}) async-start(s8[6291456]{0:T(1024)(128)(4,1)} %bitcast.523), calls=%async_computation.13 | async-start | bytes 4194304
  204.4 5.7 %slice-start.4 = ((s8[6291456]{0:T(1024)(128)(4,1)}), s8[4194304]{0:T(1024)(128)(4,1)S(1)}, s32[]{:S(2)}) async-start(s8[6291456]{0:T(1024)(128)(4,1)} %bitcast.521), calls=%async_computation.10 | async-start | bytes 8388608
  206.8 7.5 %copy-start.10 = (f32[1536,1,128]{0,2,1:T(8,128)}, f32[1536,1,128]{0,2,1:T(8,128)S(1)}, u32[]{:S(2)}) copy-start(f32[1536,1,128]{0,2,1:T(8,128)S(1)} %fusion.27) | copy-start | bytes 2359300
  206.8 5.3 %slice-start = ((s8[6291456]{0:T(1024)(128)(4,1)}), s8[4194304]{0:T(1024)(128)(4,1)S(1)}, s32[]{:S(2)}) async-start(s8[6291456]{0:T(1024)(128)(4,1)} %bitcast.517), calls=%async_computation.6 | async-start | bytes 8388608
  218.1 128.3 %reduce-scatter.3.cloned.1.call-start = ((), (), s32[]{:S(2)}) async-start(), calls=%async_computation.2 | async-start | bytes 1179648 | tf_op jit(solution)/shard_map/reduce_scatter | solution.py:138
  218.2 9.1 %slice-start.2 = ((s8[6291456]{0:T(1024)(128)(4,1)}), s8[4194304]{0:T(1024)(128)(4,1)S(1)}, s32[]{:S(2)}) async-start(s8[6291456]{0:T(1024)(128)(4,1)} %bitcast.519), calls=%async_computation.8 | async-start | bytes 8388608
  221.4 9.8 %copy-start.20 = (f32[1536,1,128]{0,2,1:T(8,128)}, f32[1536,1,128]{0,2,1:T(8,128)S(1)}, u32[]{:S(2)}) copy-start(f32[1536,1,128]{0,2,1:T(8,128)S(1)} %fusion.41) | copy-start | bytes 2359300
  221.4 5.8 %slice-start.3 = ((s8[6291456]{0:T(1024)(128)(4,1)}), s8[2097152]{0:T(1024)(128)(4,1)S(1)}, s32[]{:S(2)}) async-start(s8[6291456]{0:T(1024)(128)(4,1)} %bitcast.519), calls=%async_computation.9 | async-start | bytes 4194304
  (27 other events, 85.9 us)
Sparse Core Ops, SparseCore 0:
  10.3 39.7 all-gather.6
  52.4 43.2 all-gather.8
  218.2 37.3 reduce-scatter.4
  258.6 40.8 reduce-scatter.2
where the time goes:
time: 354 us; the launch traced here: 353 us
  blocking collectives  226 us (64%)
  matrix products  58.6 us (17%)
  local copies, waits for them, and re-layouts  29.3 us (8%)
  other arithmetic  22.8 us (6%)
  between operations  16 us (5%)
    unnamed x1, blocking collectives  90.5 us
    all_gather x1, blocking collectives, shards(): lax.all_gather(pack_key, 'resp', axis=0, tiled=True)  46.6 us
    all_gather x1, blocking collectives, shards(): lax.all_gather(pack_value, 'resp', axis=0, tiled=True)  43 us
    all_gather x1, blocking collectives, shards(): lax.all_gather(block_key, 'ctx', axis=0, tiled=True)  23.1 us
    all_gather x1, blocking collectives, shards(): lax.all_gather(block_value, 'ctx', axis=0, tiled=True)  22.9 us
    dot_general x8, matrix products, attend(): jnp.einsum('rgd,jd->grj', query_heads[:, kv_head], key_heads[:, kv_head],...  15.4 us
    dot_general x8, matrix products, attend(): jnp.einsum('rgd,jd->grj', grad_heads[:, kv_head], value_heads[:, kv_head]...  13.7 us
    unnamed x105, local copies, waits for them, and re-layouts  12.9 us
  transfers between devices with their start and end apart: 4, of which 0 were waited for; matrix products, arithmetic and copies ran while one was open for 22% of the time, Pallas kernels for 0%

commit v1 on v0

v1 whole, which is shorter than its diff:
```python
import functools
import math

import jax
import jax.numpy as jnp
from jax import lax
from jax.experimental import pallas as pl
from jax.experimental.pallas import tpu as pltpu
from jax.sharding import PartitionSpec as P

bf, f32 = jnp.bfloat16, jnp.float32
SCALE = 128 ** -0.5
C2 = SCALE * math.log2(math.e)
NEG = -1e30

def dot_t(a, b):
    return lax.dot_general(a, b, (((1,), (1,)), ((), ())), preferred_element_type=f32)
def dot_0(a, b):
    return lax.dot_general(a, b, (((0,), (0,)), ((), ())), preferred_element_type=f32)
def dot(a, b):
    return jnp.dot(a, b, preferred_element_type=f32)

def kernel(CH, DQ, sc_ref, q_ref, g_ref, o_ref, ko_ref, vo_ref, km_ref, vm_ref, kx_ref, vx_ref, pq_ref, pg_ref, po_ref,
           dq_ref, down_ref, dm_ref, dx_ref, pdq_ref,
           bias_ref, pbias_ref, k_ref, v_ref, kt_ref, qs_ref, gs_ref, dl_ref, dk_ref, dv_ref):
    h = pl.program_id(0)
    ctx, core, live, lo, hi, row0, split = [sc_ref[i] for i in range(7)]

    @pl.when(h == 0)
    def _():
        i = lax.broadcasted_iota(jnp.int32, (512, 128), 0)
        half, i = i >> 8, i & 255
        c = (core + half) & 1
        pos = (i >> 5) * 64 + ((i & 31) >> 1) * 4 + c * 2 + (i & 1)
        bias_ref[0:512] = jnp.where((pos >= lo) & (pos < hi), 0.0, NEG)
        u = lax.broadcasted_iota(jnp.int32, (1024, 128), 0)
        r = lax.broadcasted_iota(jnp.int32, (1024, 128), 1)
        bias_ref[512:1536] = jnp.where(u <= ctx * 128 + r, 0.0, NEG)
        prow = row0 + (lax.broadcasted_iota(jnp.int32, (512, 128), 1) & 1)
        seen = (pos <= prow) & ((pos >= split) == (prow >= split))
        pbias_ref[...] = jnp.where(seen, 0.0, NEG)

    k_ref[0:256] = km_ref[...]; k_ref[256:512] = kx_ref[...]; k_ref[512:] = ko_ref[...]
    v_ref[0:256] = vm_ref[...]; v_ref[256:512] = vx_ref[...]; v_ref[512:] = vo_ref[...]
    if DQ == 0:
        kt_ref[...] = k_ref[...].T
    rr = lax.broadcasted_iota(jnp.int32, (128, 128), 0)
    ones = jnp.ones((8, 256), bf)
    for g in range(8):
        s = slice(g * 128, g * 128 + 128)
        qs_ref[s] = q_ref[:, s]
        gg = jnp.where(rr < live, g_ref[:, s].astype(f32), 0.0)
        gs_ref[s] = gg.astype(bf)
        prod = gg * o_ref[:, s].astype(f32)
        ph = prod.astype(bf)
        pl_ = (prod - ph.astype(f32)).astype(bf)
        dl_ref[:, s] = dot_t(ones, jnp.concatenate([ph, pl_], axis=1))
    zero = jnp.zeros((112, 128), f32)
    def rows16(ref):
        x = ref[...].astype(f32)
        return jnp.concatenate([x[:, g * 128:g * 128 + 128] for g in range(8)] + [zero], axis=0)
    pq, pg, po = rows16(pq_ref), rows16(pg_ref), rows16(po_ref)
    prod = pg * po
    ph = prod.astype(bf)
    pl_ = (prod - ph.astype(f32)).astype(bf)
    pdl = dot_t(ones, jnp.concatenate([ph, pl_], axis=1))[0:1]
    pqb, pgb = pq.astype(bf), pg.astype(bf)

    def block(nk, K, V, bias, Q, G, delta):
        S = dot_t(K, Q) + bias
        m = jnp.max(S, axis=0, keepdims=True) * C2
        e = jnp.exp2(S * C2 - m)
        inv = 1.0 / jnp.sum(e, axis=0, keepdims=True)
        p = e * inv
        w = p.astype(bf)
        dP = dot_t(V, G)
        ds = (p * (dP - delta)).astype(bf)
        return w, ds

    w, ds = block(512, k_ref[0:512], v_ref[0:512], pbias_ref[...], pqb, pgb, pdl)
    dv_ref[0:512] = dot(w, pgb)
    dk_ref[0:512] = dot(ds, pqb)
    pdq = (dot_0(ds, k_ref[0:512]) if DQ else dot(kt_ref[:, 0:512], ds).T) * SCALE
    for g in range(8):
        pdq_ref[:, g * 128:g * 128 + 128] = pdq[2 * g:2 * g + 2].astype(bf)
    dv_ref[512:] = jnp.zeros((1024, 128), f32)
    dk_ref[512:] = jnp.zeros((1024, 128), f32)

    def chunk(i):
        rows = pl.ds(i * CH if isinstance(i, int) else pl.multiple_of(i * CH, CH), CH)
        Q, G = qs_ref[rows], gs_ref[rows]
        bias = jnp.concatenate([bias_ref[...]] * (CH // 128), axis=1)
        w, ds = block(1536, k_ref[...], v_ref[...], bias, Q, G, dl_ref[0:1, rows])
        dv_ref[...] += dot(w, G)
        dk_ref[...] += dot(ds, Q)
        dq = (dot_0(ds, k_ref[...]) if DQ else dot(kt_ref[...], ds).T) * SCALE
        for j in range(CH // 128):
            off = i * CH + j * 128
            dq_ref[:, pl.ds(off if isinstance(i, int) else pl.multiple_of(off, 128), 128)] = dq[j * 128:j * 128 + 128].astype(bf)
    pl.loop(0, 1024 // CH)(chunk)
    for dst, sl in ((dm_ref, slice(0, 256)), (dx_ref, slice(256, 512)), (down_ref, slice(512, 1536))):
        dst[:, 0:128] = (dk_ref[sl] * SCALE).astype(bf)
        dst[:, 128:256] = dv_ref[sl].astype(bf)

def attention(sc, q, g, o, kv_own, kv_m, kv_x, pq, pg, po, CH=256, DQ=0):
    wide = lambda n: pl.BlockSpec((n, 1024), lambda h: (0, h))
    kb = lambda n: pl.BlockSpec((n, 128), lambda h: (0, h))
    vb = lambda n: pl.BlockSpec((n, 128), lambda h: (0, 4 + h))
    db = lambda n: pl.BlockSpec((n, 256), lambda h: (0, h))
    return pl.pallas_call(
        functools.partial(kernel, CH, DQ),
        grid=(4,),
        in_specs=[pl.BlockSpec(memory_space=pltpu.SMEM), wide(128), wide(128), wide(128), kb(1024), vb(1024), kb(256), vb(256), kb(256), vb(256),
                  wide(2), wide(2), wide(2)],
        out_specs=[wide(128), db(1024), db(256), db(256), wide(2)],
        out_shape=[jax.ShapeDtypeStruct((128, 4096), bf), jax.ShapeDtypeStruct((1024, 1024), bf), jax.ShapeDtypeStruct((256, 1024), bf),
                   jax.ShapeDtypeStruct((256, 1024), bf), jax.ShapeDtypeStruct((2, 4096), bf)],
        scratch_shapes=[pltpu.VMEM((1536, 128), f32), pltpu.VMEM((512, 128), f32), pltpu.VMEM((1536, 128), bf), pltpu.VMEM((1536, 128), bf),
                        pltpu.VMEM((128, 1536), bf), pltpu.VMEM((1024, 128), bf), pltpu.VMEM((1024, 128), bf), pltpu.VMEM((8, 1024), f32),
                        pltpu.VMEM((1536, 128), f32), pltpu.VMEM((1536, 128), f32)],
        compiler_params=pltpu.CompilerParams(vmem_limit_bytes=48 * 1024 * 1024),
        cost_estimate=pl.CostEstimate(flops=8 * 10**9, bytes_accessed=12 * 2**20, transcendentals=6 * 10**6),
    )(sc, q, g, o, kv_own, kv_own, kv_m, kv_m, kv_x, kv_x, pq, pg, po)


YZ = [[c + 2 * i for i in range(16)] for c in range(2)]
SWAP = [(i, i ^ 1) for i in range(32)]


def halves(total):
    rows = total.shape[0]
    split = total.reshape(rows, 4, 2, 128)
    return split[:, :, 0].reshape(rows, 512), split[:, :, 1].reshape(rows, 512)


def spread(block, axis, count, groups=None):
    copies = jnp.broadcast_to(block[None], (count,) + block.shape)
    got = lax.all_to_all(copies, axis, 0, 0, tiled=True, axis_index_groups=groups)
    return got.reshape((count * block.shape[0],) + block.shape[1:])


def collect(parts, axis, count, groups=None):
    rows = parts.shape[0] // count
    got = lax.all_to_all(parts.reshape((count, rows) + parts.shape[1:]), axis, 0, 0, tiled=True, axis_index_groups=groups)
    return jnp.sum(got.astype(f32), axis=0)


def shards(
    resp_query, resp_key, resp_value, resp_out, resp_grad,
    pack_query, pack_key, pack_value, pack_out, pack_grad,
    resp_length, prompt_id, pack_offset,
):
    ctx = lax.axis_index("ctx")
    resp = lax.axis_index("resp")
    middle = pack_offset[1]
    first = prompt_id[0] == 0
    scalars = jnp.stack([
        ctx, resp & 1, resp_length[0] - ctx * 128,
        jnp.where(first, 0, middle), jnp.where(first, middle, 512),
        (ctx * 32 + resp) * 2, middle,
    ]).astype(jnp.int32)
    own = spread(jnp.concatenate([resp_key[0], resp_value[0]], axis=1), "ctx", 8)
    pack = spread(jnp.concatenate([pack_key, pack_value], axis=1), "resp", 16, YZ)
    mine = spread(pack, "ctx", 8)
    other = lax.ppermute(mine, "resp", SWAP)
    dq, down, dmine, dother, pdq = attention(
        scalars, resp_query[0], resp_grad[0], resp_out[0], own, mine, other, pack_query, pack_grad, pack_out
    )
    own_total = collect(down, "ctx", 8).astype(bf)
    both = (dmine.astype(f32) + lax.ppermute(dother, "resp", SWAP).astype(f32)).astype(bf)
    group = collect(both, "ctx", 8).astype(bf)
    total = collect(group, "resp", 16, YZ).astype(bf)
    own_key, own_value = halves(own_total)
    block_key, block_value = halves(total)
    return dq[None], own_key[None], own_value[None], pdq, block_key, block_value


def solution(mesh):
    long = P("resp", "ctx", None)
    pack = P(("ctx", "resp"), None)
    return jax.shard_map(
        shards,
        mesh=mesh,
        in_specs=(long,) * 5 + (pack,) * 5 + (P("resp"), P("resp"), P()),
        out_specs=(long,) * 3 + (pack,) * 3,
        check_vma=False,
    )
```

time: 354 us -> 167 us (0.47)
  blocking collectives: 226 us -> 45.3 us
  matrix products: 58.6 us -> 0 us
  waiting for transfers between devices: 0.09 us -> 54.9 us
  Pallas kernels: 0 us -> 36.7 us
  local copies, waits for them, and re-layouts: 29.3 us -> 7.45 us
  other arithmetic: 22.8 us -> 2.39 us
  starting transfers between devices: 0.16 us -> 16.2 us
  between operations: 16 us -> 3.37 us
    all_gather x4 -> x0, blocking collectives: 136 us -> none  [the longest x1 46.6 us: shards(): lax.all_gather(pack_key, 'resp', axis=0, tiled=True)]
    unnamed x1 -> x0, blocking collectives: 90.5 us -> none
    dot_general x40 -> x0, matrix products: 58.6 us -> none  [the longest x8 15.4 us: attend(): jnp.einsum('rgd,jd->grj', query_heads[:, kv_head], key_heads[:, kv_head],...]
    all_to_all x0 -> x3, waiting for transfers between devices: none -> 53.3 us  [the longest x2 27 us: spread(): lax.all_to_all(copies, axis, 0, 0, tiled=True, axis_index_groups=groups)]
    all_to_all x0 -> x3, blocking collectives: none -> 45.3 us  [the longest x2 24.9 us: collect(): lax.all_to_all(parts.reshape((count, rows) + parts.shape[1:]), axis, 0, 0...]
    pallas_call x0 -> x1, Pallas kernels: none -> 36.7 us  [attention(): pl.pallas_call(functools.partial(kernel, CH, DQ), grid=(4,), in_specs=[pl...]
    all_to_all x0 -> x3, starting transfers between devices: none -> 12.2 us  [the longest x2 8.62 us: spread(): lax.all_to_all(copies, axis, 0, 0, tiled=True, axis_index_groups=groups)]
    unnamed x105 -> x16, local copies, waits for them, and re-layouts: 12.9 us -> 2.79 us
  transfers between devices with their start and end apart: 4 -> 5, of which waited for: 0 -> 4; matrix products, arithmetic and copies ran while one was open for 22% -> 2% of each run, Pallas kernels for 0% -> 0%
where the time goes in v1:
time: 167 us; the launch traced here: 166 us
  waiting for transfers between devices  54.9 us (33%)
  blocking collectives  45.3 us (27%)
  Pallas kernels  36.7 us (22%)
  starting transfers between devices  16.2 us (10%)
  local copies, waits for them, and re-layouts  7.45 us (4%)
  between operations  3.37 us (2%)
  other arithmetic  2.39 us (1%)
    pallas_call x1, Pallas kernels, attention(): pl.pallas_call(functools.partial(kernel, CH, DQ), grid=(4,), in_specs=[pl...  36.7 us
    all_to_all x2, waiting for transfers between devices, spread(): lax.all_to_all(copies, axis, 0, 0, tiled=True, axis_index_groups=groups)  27 us
    all_to_all x1, waiting for transfers between devices, collect(): lax.all_to_all(parts.reshape((count, rows) + parts.shape[1:]), axis, 0, 0...  26.3 us
    all_to_all x2, blocking collectives, collect(): lax.all_to_all(parts.reshape((count, rows) + parts.shape[1:]), axis, 0, 0...  24.9 us
    all_to_all x1, blocking collectives, spread(): lax.all_to_all(copies, axis, 0, 0, tiled=True, axis_index_groups=groups)  20.4 us
    all_to_all x2, starting transfers between devices, spread(): lax.all_to_all(copies, axis, 0, 0, tiled=True, axis_index_groups=groups)  8.62 us
    all_to_all x1, starting transfers between devices, collect(): lax.all_to_all(parts.reshape((count, rows) + parts.shape[1:]), axis, 0, 0...  3.6 us
  transfers between devices with their start and end apart: 5, of which 4 were waited for; matrix products, arithmetic and copies ran while one was open for 2% of the time, Pallas kernels for 0%

profile of v1, /device:TPU:1, one launch (start us, length us, event | category | flops | bytes accessed | tf_op | source)
XLA Modules:
  0.0 166.2 jit_solution(15040472842638844359)
XLA Ops:
  0.6 0.7 pad_maximum_fusion.1
  1.4 20.4 %all_to_all.30 = bf16[16,2,1024]{2,1,0:T(2,128)(2,1)S(1)} all-to-all(bf16[16,2,1024]{2,1,0:T(2,128)(2,1)S(1)} %broadcast_in_dim.11), channel_id=1, replica_groups={{0,2,4,6,8,10,12,14,16,18,20,22,24,26,28,30},{1,3,5,7,9,11,13,15,17,19,..., dimensions={0} | all-to-all | bytes 131072 | tf_op jit(solution)/shard_map/all_to_all | solution.py:138
  21.8 0.9 broadcast_in_dim.25
  22.7 4.1 %all-to-all-start.2 = ((bf16[8,32,1024]{2,1,0:T(8,128)(2,1)}), bf16[8,32,1024]{2,1,0:T(8,128)(2,1)S(1)}, u32[]{:S(2)}, u32[]{:S(2)}) async-start(bf16[8,32,1024]{2,1,0:T(8,128)(2,1)} %broadcast_in_dim.25), calls=%async_computation.2 | async-start | bytes 1048576 | tf_op jit(solution)/shard_map/all_to_all | solution.py:138
  26.8 1.0 pad_maximum_fusion
  27.8 7.0 %all-to-all-done.2 = bf16[8,32,1024]{2,1,0:T(8,128)(2,1)S(1)} async-done(((bf16[8,32,1024]{2,1,0:T(8,128)(2,1)}), bf16[8,32,1024]{2,1,0:T(8,128)(2,1)S(1)}, u32[]{:S(2)}, u32[]{:S(2)}) %all-to-all-start.2) | async-done | bytes 524320 | tf_op jit(solution)/shard_map/all_to_all | solution.py:138
  34.9 1.6 broadcast_in_dim.10
  36.5 4.5 %all-to-all-start = ((bf16[8,128,1024]{2,1,0:T(8,128)(2,1)}), bf16[8,128,1024]{2,1,0:T(8,128)(2,1)}, u32[]{:S(2)}, u32[]{:S(2)}) async-start(bf16[8,128,1024]{2,1,0:T(8,128)(2,1)} %broadcast_in_dim.10), calls=%async_computation | async-start | bytes 4194304 | tf_op jit(solution)/shard_map/all_to_all | solution.py:138
  41.0 3.1 %collective-permute-start = (bf16[256,1024]{1,0:T(8,128)(2,1)S(1)}, bf16[256,1024]{1,0:T(8,128)(2,1)S(1)}, u32[]{:S(2)}, u32[]{:S(2)}) collective-permute-start(bf16[256,1024]{1,0:T(8,128)(2,1)S(1)} %bitcast.25), channel_id=1, source_target_pairs={{0,1},{1,0},{2,3},{3,2},{4,5},{5,4},{6,7},{7,6},{8,9},{9,8},{10,11... | collective-permute-start | bytes 1572872 | tf_op jit(solution)/shard_map/ppermute | solution.py:165
  45.4 0.6 slice.15
  47.3 0.7 stack.21.sc_ref
  48.0 20.0 %all-to-all-done = bf16[8,128,1024]{2,1,0:T(8,128)(2,1)} async-done(((bf16[8,128,1024]{2,1,0:T(8,128)(2,1)}), bf16[8,128,1024]{2,1,0:T(8,128)(2,1)}, u32[]{:S(2)}, u32[]{:S(2)}) %all-to-all-start) | async-done | bytes 2097184 | tf_op jit(solution)/shard_map/all_to_all | solution.py:138
  68.1 1.2 copy-done.2
  69.3 36.7 %shard_map.172 = (bf16[128,4096]{1,0:T(8,128)(2,1)}, bf16[1024,1024]{1,0:T(8,128)(2,1)}, bf16[256,1024]{1,0:T(8,128)(2,1)S(1)}, bf16[256,1024]{1,0:T(8,128)(2,1)S(1)}, bf16[2,4096]{1,0:T(2,128)(2,1)}) custom-call(s32[7]{0:T(128)S(1)} %stack.21.sc_ref, bf16[128,4096]{1,0:T(8,128)(2,1)S(1)} %bitcast.28, bf16[128,4096]{1,0:T(8,128)(2,1)S(1)} %bitcast.29, ...), custom_call_target="tpu_custom_call" | custom-call | flops 8000000000 | bytes 12582912 | tf_op jit(solution)/shard_map/pallas_call | solution.py:110
  105.9 0.9 collective-permute-start.1
  106.8 1.5 collective-permute-done.1
  108.5 12.6 %all_to_all.31 = bf16[8,32,1024]{2,1,0:T(8,128)(2,1)S(1)} all-to-all(bf16[8,32,1024]{2,1,0:T(8,128)(2,1)S(1)} %bitcast.31), channel_id=1, replica_groups=mesh['ctx'=8,'resp'=32] {'ctx'}, dimensions={0} | all-to-all | bytes 1048576 | tf_op jit(solution)/shard_map/all_to_all | solution.py:144
  121.3 12.2 %all_to_all.32 = bf16[16,2,1024]{2,1,0:T(2,128)(2,1)S(1)} all-to-all(bf16[16,2,1024]{2,1,0:T(2,128)(2,1)S(1)} %reshape.49), channel_id=1, replica_groups={{0,2,4,6,8,10,12,14,16,18,20,22,24,26,28,30},{1,3,5,7,9,11,13,15,17,19,..., dimensions={0} | all-to-all | bytes 131072 | tf_op jit(solution)/shard_map/all_to_all | solution.py:144
  133.5 3.6 %all-to-all-start.3 = ((bf16[8,128,1024]{2,1,0:T(8,128)(2,1)}), bf16[8,128,1024]{2,1,0:T(8,128)(2,1)S(1)}, u32[]{:S(2)}, u32[]{:S(2)}) async-start(bf16[8,128,1024]{2,1,0:T(8,128)(2,1)} %bitcast.32), calls=%async_computation.3 | async-start | bytes 4194304 | tf_op jit(solution)/shard_map/all_to_all | solution.py:144
  137.2 0.6 copy_bitcast_fusion
  137.8 26.3 %all-to-all-done.3 = bf16[8,128,1024]{2,1,0:T(8,128)(2,1)S(1)} async-done(((bf16[8,128,1024]{2,1,0:T(8,128)(2,1)}), bf16[8,128,1024]{2,1,0:T(8,128)(2,1)S(1)}, u32[]{:S(2)}, u32[]{:S(2)}) %all-to-all-start.3) | async-done | bytes 2097184 | tf_op jit(solution)/shard_map/all_to_all | solution.py:144
  164.1 0.4 reduce_sum.36
  164.7 0.8 copy.32
  165.4 0.8 copy.31
  (24 shorter events, 0.7 us)
Async XLA Ops:
  22.7 12.2 %all-to-all-start.2 = ((bf16[8,32,1024]{2,1,0:T(8,128)(2,1)}), bf16[8,32,1024]{2,1,0:T(8,128)(2,1)S(1)}, u32[]{:S(2)}, u32[]{:S(2)}) async-start(bf16[8,32,1024]{2,1,0:T(8,128)(2,1)} %broadcast_in_dim.25), calls=%async_computation.2 | async-start | bytes 1048576 | tf_op jit(solution)/shard_map/all_to_all | solution.py:138
  36.4 8.9 %copy-start.6 = (s32[3]{0:T(128)S(1)}, s32[3]{0:T(128)}, u32[]{:S(2)}) copy-start(s32[3]{0:T(128)} %param.25) | copy-start | bytes 40
  36.4 31.6 %copy-start = (bf16[1,128,4096]{2,1,0:T(8,128)(2,1)S(1)}, bf16[1,128,4096]{2,1,0:T(8,128)(2,1)}, u32[]{:S(2)}) copy-start(bf16[1,128,4096]{2,1,0:T(8,128)(2,1)} %param.13) | copy-start | bytes 3145732
  36.4 31.6 %copy-start.1 = (bf16[1,128,4096]{2,1,0:T(8,128)(2,1)S(1)}, bf16[1,128,4096]{2,1,0:T(8,128)(2,1)}, u32[]{:S(2)}) copy-start(bf16[1,128,4096]{2,1,0:T(8,128)(2,1)} %param.17) | copy-start | bytes 3145732
  36.4 31.6 %copy-start.3 = (bf16[2,4096]{1,0:T(2,128)(2,1)S(1)}, bf16[2,4096]{1,0:T(2,128)(2,1)}, u32[]{:S(2)}) copy-start(bf16[2,4096]{1,0:T(2,128)(2,1)} %pq_ref.1) | copy-start | bytes 49156
  36.4 31.6 %copy-start.4 = (bf16[2,4096]{1,0:T(2,128)(2,1)S(1)}, bf16[2,4096]{1,0:T(2,128)(2,1)}, u32[]{:S(2)}) copy-start(bf16[2,4096]{1,0:T(2,128)(2,1)} %pg_ref.1) | copy-start | bytes 49156
  36.5 31.6 %copy-start.5 = (bf16[2,4096]{1,0:T(2,128)(2,1)S(1)}, bf16[2,4096]{1,0:T(2,128)(2,1)}, u32[]{:S(2)}) copy-start(bf16[2,4096]{1,0:T(2,128)(2,1)} %po_ref.1) | copy-start | bytes 49156
  36.5 31.5 %all-to-all-start = ((bf16[8,128,1024]{2,1,0:T(8,128)(2,1)}), bf16[8,128,1024]{2,1,0:T(8,128)(2,1)}, u32[]{:S(2)}, u32[]{:S(2)}) async-start(bf16[8,128,1024]{2,1,0:T(8,128)(2,1)} %broadcast_in_dim.10), calls=%async_computation | async-start | bytes 4194304 | tf_op jit(solution)/shard_map/all_to_all | solution.py:138
  41.0 7.1 %collective-permute-start = (bf16[256,1024]{1,0:T(8,128)(2,1)S(1)}, bf16[256,1024]{1,0:T(8,128)(2,1)S(1)}, u32[]{:S(2)}, u32[]{:S(2)}) collective-permute-start(bf16[256,1024]{1,0:T(8,128)(2,1)S(1)} %bitcast.25), channel_id=1, source_target_pairs={{0,1},{1,0},{2,3},{3,2},{4,5},{5,4},{6,7},{7,6},{8,9},{9,8},{10,11... | collective-permute-start | bytes 1572872 | tf_op jit(solution)/shard_map/ppermute | solution.py:165
  68.0 1.2 copy-start.2
  105.9 2.4 %collective-permute-start.1 = (bf16[256,1024]{1,0:T(8,128)(2,1)S(1)}, bf16[256,1024]{1,0:T(8,128)(2,1)S(1)}, u32[]{:S(2)}, u32[]{:S(2)}) collective-permute-start(bf16[256,1024]{1,0:T(8,128)(2,1)S(1)} %get-tuple-element.15), channel_id=1, source_target_pairs={{0,1},{1,0},{2,3},{3,2},{4,5},{5,4},{6,7},{7,6},{8,9},{9,8},{10,11... | collective-permute-start | bytes 1572872 | tf_op jit(solution)/shard_map/ppermute | solution.py:170
  133.5 30.6 %all-to-all-start.3 = ((bf16[8,128,1024]{2,1,0:T(8,128)(2,1)}), bf16[8,128,1024]{2,1,0:T(8,128)(2,1)S(1)}, u32[]{:S(2)}, u32[]{:S(2)}) async-start(bf16[8,128,1024]{2,1,0:T(8,128)(2,1)} %bitcast.32), calls=%async_computation.3 | async-start | bytes 4194304 | tf_op jit(solution)/shard_map/all_to_all | solution.py:144
